TPU v7x, 512 devices: a whole 4x8x8 slice. The times are simulated.
512 devices in a mesh: bucket: 16 (over x_hi, y), shard: 32 (over z, x_lo, core).
Axes of the slice: x: 4 (x_hi: 2, x_lo: 2; x = x_hi * 2 + x_lo), y: 8, z: 8, core: 2. Of those that a mesh axis runs over, the one named last changes fastest.
Arguments:
- source_slab: float32 [524288, 256], P(('bucket', 'shard')), may hold values from -1.5 to 1.5
- source_state: float32 [524288], P(('bucket', 'shard')), may hold values from 0.001 to 0.1
- dest_slab: float32 [524288, 256], P(('bucket', 'shard')), may hold values from -1.5 to 1.5
- dest_state: float32 [524288], P(('bucket', 'shard')), may hold values from 0.001 to 0.1
- source_rows: int32 [524288], P(('bucket', 'shard')), may hold values from 0 to 1023
- target_owner: int32 [524288, 1], P(('bucket', 'shard')), may hold values from 0 to 31; in each aligned block of 1024 rows (0 to 1023, 1024 to 2047, ...) at most 48 rows name the same one
- target_rows: int32 [524288], P(('bucket', 'shard')), may hold values from 0 to 1023
- negative_owner: int32 [1048576, 1], P(('bucket', 'shard')), may hold values from 0 to 31; in each aligned block of 2048 rows (0 to 2047, 2048 to 4095, ...) at most 96 rows name the same one
- negative_rows: int32 [1048576], P(('bucket', 'shard')), may hold values from 0 to 1023
- edge_count: int32 [512], P(('bucket', 'shard')), may hold values from 256 to 1024
- matching: int32 [16], replicated, may hold values from 0 to 15, as said below
Outputs:
- updated_source: float32 [524288, 256], P(('bucket', 'shard'))
- updated_source_state: float32 [524288], P(('bucket', 'shard'))
- incoming_dest: float32 [524288, 256], P(('bucket', 'shard'))
- incoming_dest_state: float32 [524288], P(('bucket', 'shard'))
Inputs may be any that keep to these rules, and one draw needn't show every extreme that they name: `target_owner`: among the edges of one index pair, at most 48 name one owner. `negative_owner`: among the negatives of one index pair, at most 96 name one owner. matching[g] = g XOR m for one m from 1 to 15, the same for all g.
All inputs are finite; a program needn't handle non-finite values.
Results may differ from a plain program's by a relative error of at most 0.0023.
Values may be sent and summed in bfloat16 or wider, within the bound.
A program may use at most 64 MiB of HBM per device.

v0:
```python
import jax
import jax.numpy as jnp
from jax import lax
from jax.sharding import PartitionSpec as P

learn_rate = 0.1
epsilon = 1e-06


def from_partner(shard, axis, stride):
    return lax.ppermute(shard, axis, [(i, i ^ 1 << stride) for i in range(lax.axis_size(axis))])


def adagrad_rows(table_rows, row_state, row_grad):
    fresh_state = row_state + jnp.mean(row_grad * row_grad, axis=1)
    return (
        table_rows - learn_rate * row_grad / (jnp.sqrt(fresh_state)[:, None] + epsilon),
        fresh_state,
    )


def slot_of(owner_ids, shards, offset):
    onehot = (owner_ids[:, None] == jnp.arange(shards, dtype=jnp.int32)[None, :]).astype(jnp.int32)
    before = jnp.cumsum(onehot, axis=0) - onehot
    return jnp.sum(before * onehot, axis=1) + offset


def carry_over(table_rows, row_state, matching):
    partner_mask = matching[0]
    bit_levels = lax.axis_size("bucket").bit_length() - 1
    for bit_level in range(bit_levels):
        flipped = jnp.bitwise_and(jnp.right_shift(partner_mask, bit_level), 1) == 1
        partner = from_partner((table_rows, row_state), "bucket", bit_level)
        table_rows = jnp.where(flipped, partner[0], table_rows)
        row_state = jnp.where(flipped, partner[1], row_state)
    return (table_rows, row_state)


def per_device(
    source_slab,
    source_state,
    dest_slab,
    dest_state,
    source_rows,
    target_owner,
    target_rows,
    negative_owner,
    negative_rows,
    edge_count,
    matching,
):
    shards = lax.axis_size("shard")
    edge_total = source_rows.shape[0]
    neg_total = negative_rows.shape[0]
    features = source_slab.shape[1]
    edge_slots = 3 * edge_total // (2 * shards)
    slot_total = edge_slots + 3 * neg_total // (2 * shards)
    edge_owner = target_owner[:, 0]
    neg_owner = negative_owner[:, 0]
    edge_place = slot_of(edge_owner, shards, 0)
    neg_place = slot_of(neg_owner, shards, edge_slots)
    request = jnp.zeros((shards, slot_total), jnp.int32)
    request = (
        request.at[edge_owner, edge_place]
        .set(target_rows)
        .at[neg_owner, neg_place]
        .set(negative_rows)
    )
    asked_rows = lax.all_to_all(request, "shard", split_axis=0, concat_axis=0, tiled=True)
    looked_up = dest_slab[asked_rows].astype(jnp.bfloat16)
    fetched = lax.all_to_all(looked_up, "shard", split_axis=0, concat_axis=0, tiled=True)
    targets = fetched[edge_owner, edge_place]
    negatives = fetched[neg_owner, neg_place]
    sources = source_slab[source_rows].astype(jnp.bfloat16)
    live_mask = (jnp.arange(edge_total, dtype=jnp.int32) < edge_count[0]).astype(jnp.float32)
    positive = jnp.einsum("ed,ed->e", sources, targets, preferred_element_type=jnp.float32)
    pos_coef = -live_mask * jax.nn.sigmoid(-positive)
    neg_weight = neg_total ** (-0.5)
    block_rows = min(512, edge_total)
    block_count = edge_total // block_rows

    def score_block(neg_accum, pieces):
        src_block, live_block = pieces
        scores = lax.dot_general(
            src_block, negatives, (((1,), (1,)), ((), ())), preferred_element_type=jnp.float32
        )
        weights = (live_block[:, None] * neg_weight * jax.nn.sigmoid(scores)).astype(jnp.bfloat16)
        neg_accum = neg_accum + lax.dot_general(
            weights, src_block, (((0,), (0,)), ((), ())), preferred_element_type=jnp.float32
        )
        return (neg_accum, jnp.dot(weights, negatives, preferred_element_type=jnp.float32))

    neg_grad, block_grads = lax.scan(
        score_block,
        jnp.zeros((neg_total, features), jnp.float32),
        (
            sources.reshape(block_count, block_rows, features),
            live_mask.reshape(block_count, block_rows),
        ),
    )
    source_grad = pos_coef[:, None] * targets.astype(jnp.float32) + block_grads.reshape(
        edge_total, features
    )
    target_grad = (pos_coef[:, None] * sources.astype(jnp.float32)).astype(jnp.bfloat16)
    grad_buffer = jnp.zeros((shards, slot_total, features), jnp.bfloat16)
    grad_buffer = (
        grad_buffer.at[edge_owner, edge_place]
        .set(target_grad)
        .at[neg_owner, neg_place]
        .set(neg_grad.astype(jnp.bfloat16))
    )
    returned = lax.all_to_all(grad_buffer, "shard", split_axis=0, concat_axis=0, tiled=True)
    dest_grad = (
        jnp.zeros(dest_slab.shape, jnp.float32)
        .at[asked_rows.reshape(-1)]
        .add(returned.reshape(-1, features).astype(jnp.float32))
    )
    source_sum = jnp.zeros(source_slab.shape, jnp.float32).at[source_rows].add(source_grad)
    new_source, new_source_state = adagrad_rows(source_slab, source_state, source_sum)
    new_dest, new_dest_state = adagrad_rows(dest_slab, dest_state, dest_grad)
    incoming_rows, incoming_state = carry_over(new_dest, new_dest_state, matching)
    return (new_source, new_source_state, incoming_rows, incoming_state)


def solution(mesh):
    in_specs = (
        P(("bucket", "shard"), None),
        P(("bucket", "shard")),
        P(("bucket", "shard"), None),
        P(("bucket", "shard")),
        P(("bucket", "shard")),
        P(("bucket", "shard"), None),
        P(("bucket", "shard")),
        P(("bucket", "shard"), None),
        P(("bucket", "shard")),
        P(("bucket", "shard")),
        P(),
    )
    out_specs = (
        P(("bucket", "shard"), None),
        P(("bucket", "shard")),
        P(("bucket", "shard"), None),
        P(("bucket", "shard")),
    )
    return jax.shard_map(
        per_device, mesh=mesh, in_specs=in_specs, out_specs=out_specs, check_vma=False
    )
```

profile of v0, /device:TPU:6, one launch (start us, length us, event | category | flops | bytes accessed | tf_op | source)
XLA Modules:
  0.0 467.4 jit_solution(1968762129482011762)
XLA Ops:
  0.7 0.7 fusion.30
  1.4 9.0 %reduce-window.14 = s32[32,8,128]{2,1,0:T(8,128)S(1)} reduce-window(s32[32,8,128]{2,1,0:T(8,128)S(1)} %fusion.30, s32[]{:T(128)} %constant.34.clone.1), window={size=1x1x128 pad=0_0x0_0x127_0}, to_apply=%region_0.0 | reduce-window | flops 4161536 | bytes 262148 | tf_op jit(solution)/shard_map/reduce-window
  10.5 0.1 copy.15
  10.8 0.7 fusion.29
  11.6 0.7 shift-left_or_fusion.1
  12.3 0.7 and_reduce_fusion.1
  13.0 0.7 multiply_reduce_fusion.3
  13.8 0.7 fusion.26
  14.5 9.1 %reduce-window.16 = s32[32,16,128]{2,1,0:T(8,128)S(1)} reduce-window(s32[32,16,128]{2,1,0:T(8,128)S(1)} %fusion.26, s32[]{:T(128)} %constant.34.clone.1), window={size=1x1x128 pad=0_0x0_0x127_0}, to_apply=%region_4.5 | reduce-window | flops 8323072 | bytes 524292 | tf_op jit(solution)/shard_map/reduce-window.2
  23.6 0.1 slice.30
  23.7 0.2 copy.24
  24.0 0.2 reduce-window.19
  24.2 0.1 broadcast_add_fusion
  24.3 0.1 fusion.25
  24.5 0.1 and_reduce_fusion
  24.7 4.5 scatter_custom_fusion.2
  29.3 8.1 %scatter_fusion = s32[4608]{0:T(1024)S(1)} fusion(s32[4608]{0:T(1024)S(1)} %scatter_custom_fusion.2, s32[2048]{0:T(1024)S(1)} %broadcast_select_fusion.4, s32[2048]{0:T(1024)S(1)} %copy-done.8), kind=kCustom, calls=%fused_computation.7 | custom fusion | bytes 32768
  37.4 0.1 all_to_all.14
  37.5 19.1 %all_to_all.22 = s32[32,1,144]{2,1,0:T(1,128)S(1)} all-to-all(s32[32,1,144]{2,1,0:T(1,128)S(1)} %all_to_all.14), channel_id=1, replica_groups=mesh['bucket'=16,'shard'=32] {'shard'}, dimensions={0} | all-to-all | bytes 36864 | tf_op jit(solution)/shard_map/all_to_all | solution.py:69
  56.8 11.3 %gather_fusion.1 = bf16[4608,256]{1,0:T(8,128)(2,1)} fusion(f32[1024,256]{1,0:T(8,128)S(1)} %copy-done, s32[5120]{0:T(1024)S(1)} %pad_clamp_fusion), kind=kCustom, calls=%fused_computation.1 | custom fusion | bytes 4737024 | tf_op jit(solution)/shard_map/gather | solution.py:70
  68.1 5.7 %all-to-all-start.1 = ((bf16[32,144,256]{2,1,0:T(8,128)(2,1)}), bf16[32,144,256]{2,1,0:T(8,128)(2,1)}, u32[]{:S(2)}, u32[]{:S(2)}) async-start(bf16[32,144,256]{2,1,0:T(8,128)(2,1)} %bitcast.103), calls=%async_computation.1 | async-start | bytes 4718592 | tf_op jit(solution)/shard_map/all_to_all | solution.py:71
  74.5 5.8 %gather_fusion = bf16[1024,256]{1,0:T(8,128)(2,1)} fusion(f32[1024,256]{1,0:T(8,128)} %param.13, s32[1024]{0:T(1024)S(1)} %get-tuple-element.84), kind=kCustom, calls=%fused_computation | custom fusion | bytes 1052672 | tf_op jit(solution)/shard_map/gather | solution.py:74
  80.3 50.7 %all-to-all-done.1 = bf16[32,144,256]{2,1,0:T(8,128)(2,1)} async-done(((bf16[32,144,256]{2,1,0:T(8,128)(2,1)}), bf16[32,144,256]{2,1,0:T(8,128)(2,1)}, u32[]{:S(2)}, u32[]{:S(2)}) %all-to-all-start.1) | async-done | bytes 2359328 | tf_op jit(solution)/shard_map/all_to_all | solution.py:71
  131.0 35.0 %gather_fusion.3 = bf16[2048,256]{1,0:T(8,128)(2,1)} fusion(bf16[32,144,256]{2,1,0:T(8,128)(2,1)} %all-to-all-done.1, s32[2048]{0:T(1024)S(1)} %bitcast.97), kind=kCustom, calls=%fused_computation.3 | custom fusion | bytes 2113536 | tf_op jit(solution)/shard_map/gather | solution.py:73
  166.1 11.2 %while.13 = (s32[]{:T(128)}, f32[2048,256]{1,0:T(8,128)S(1)}, f32[2,512,256]{2,1,0:T(8,128)}, f32[2,512]{1,0:T(2,128)S(1)}, bf16[2,512,256]{2,1,0:T(8,128)(2,1)}...) while((s32[]{:T(128)}, f32[2048,256]{1,0:T(8,128)S(1)}, f32[2,512,256]{2,1,0:T(8,128)}, ...), condition=%wide.region_9.10_spmd.clone, body=%wide.region_8.9_spmd.clone.sunk | while | flops 1616904704 | bytes 28317928 | solution.py:93
  166.1 2.8 multiply_convert_fusion.2
  169.0 0.7 fusion.52
  169.7 0.3 copy-done.2
  170.0 1.7 convolution_add_fusion.2
  171.7 2.8 multiply_convert_fusion.2
  174.6 0.7 fusion.52
  175.3 0.3 copy-done.2
  175.6 1.7 convolution_add_fusion.2
  177.3 17.8 %gather_fusion.2 = bf16[1024,256]{1,0:T(8,128)(2,1)} fusion(bf16[32,144,256]{2,1,0:T(8,128)(2,1)} %all-to-all-done.1, s32[1024]{0:T(1024)S(1)} %bitcast.98), kind=kCustom, calls=%fused_computation.2 | custom fusion | bytes 1056768 | tf_op jit(solution)/shard_map/gather | solution.py:72
  195.1 1.4 fusion.14
  196.6 7.6 %scatter_custom_fusion.4 = bf16[4608,256]{1,0:T(8,128)(2,1)} fusion(s32[1024]{0:T(1024)S(1)} %broadcast_select_fusion.5, bf16[]{:T(256)} %constant.80.clone.1, bf16[1024,256]{1,0:T(8,128)(2,1)} %bitcast.101, f32[1024]{0:T(1024)S(1)} %divide_multiply_fusion), kind=kCustom, calls=%fused_computation.26 | custom fusion | flops 786432 | bytes 2887682
  204.2 12.7 %scatter_custom_fusion.5 = bf16[4608,256]{1,0:T(8,128)(2,1)} fusion(bf16[4608,256]{1,0:T(8,128)(2,1)} %scatter_custom_fusion.4, s32[2048]{0:T(1024)S(1)} %broadcast_select_fusion.4, f32[2048,256]{1,0:T(8,128)S(1)} %get-tuple-element.38), kind=kCustom, calls=%fused_computation.34 | custom fusion | flops 524288 | bytes 4456448
  216.8 4.8 %all-to-all-start.2 = ((bf16[32,144,256]{2,1,0:T(8,128)(2,1)}), bf16[32,144,256]{2,1,0:T(8,128)(2,1)}, u32[]{:S(2)}, u32[]{:S(2)}) async-start(bf16[32,144,256]{2,1,0:T(8,128)(2,1)} %bitcast.102), calls=%async_computation.2 | async-start | bytes 4718592 | tf_op jit(solution)/shard_map/all_to_all | solution.py:112
  221.9 57.0 %all-to-all-done.2 = bf16[32,144,256]{2,1,0:T(8,128)(2,1)} async-done(((bf16[32,144,256]{2,1,0:T(8,128)(2,1)}), bf16[32,144,256]{2,1,0:T(8,128)(2,1)}, u32[]{:S(2)}, u32[]{:S(2)}) %all-to-all-start.2) | async-done | bytes 2359328 | tf_op jit(solution)/shard_map/all_to_all | solution.py:112
  278.8 23.7 %scatter_custom_fusion.1 = f32[1024,256]{1,0:T(8,128)S(1)} fusion(s32[4608]{0:T(1024)S(1)} %fusion.32, bf16[4608,256]{1,0:T(8,128)(2,1)} %bitcast.28, f32[]{:T(128)} %constant.32.clone.1), kind=kCustom, calls=%fused_computation.21 | custom fusion | flops 2359296 | bytes 3407876 | tf_op jit(solution)/shard_map/scatter-add | solution.py:116
  302.5 0.2 multiply_reduce_fusion
  302.8 0.2 divide_subtract_fusion
  303.0 3.4 collective-permute-start
  306.5 23.0 %collective-permute-done = f32[1024,256]{1,0:T(8,128)S(1)} collective-permute-done((f32[1024,256]{1,0:T(8,128)S(1)}, f32[1024,256]{1,0:T(8,128)S(1)}, u32[]{:S(2)}, u32[]{:S(2)}) %collective-permute-start) | collective-permute-done | bytes 1048608 | tf_op jit(solution)/shard_map/ppermute | solution.py:11
  329.5 0.1 broadcast_select_fusion
  329.7 4.9 %collective-permute-start.1 = (f32[1024,256]{1,0:T(8,128)S(1)}, f32[1024,256]{1,0:T(8,128)S(1)}, u32[]{:S(2)}, u32[]{:S(2)}) collective-permute-start(f32[1024,256]{1,0:T(8,128)S(1)} %broadcast_select_fusion), channel_id=1, source_target_pairs={{0,64},{32,96},{64,0},{96,32},{128,192},{160,224},{192,128},{224,1... | collective-permute-start | bytes 3145736 | tf_op jit(solution)/shard_map/ppermute | solution.py:11
  334.5 46.3 %collective-permute-done.1 = f32[1024,256]{1,0:T(8,128)S(1)} collective-permute-done((f32[1024,256]{1,0:T(8,128)S(1)}, f32[1024,256]{1,0:T(8,128)S(1)}, u32[]{:S(2)}, u32[]{:S(2)}) %collective-permute-start.1) | collective-permute-done | bytes 1048608 | tf_op jit(solution)/shard_map/ppermute | solution.py:11
  380.8 0.1 broadcast_select_fusion.1
  381.0 8.3 %collective-permute-start.2 = (f32[1024,256]{1,0:T(8,128)S(1)}, f32[1024,256]{1,0:T(8,128)}, u32[]{:S(2)}, u32[]{:S(2)}) collective-permute-start(f32[1024,256]{1,0:T(8,128)S(1)} %broadcast_select_fusion.1), channel_id=1, source_target_pairs={{0,128},{32,160},{64,192},{96,224},{128,0},{160,32},{192,64},{224,... | collective-permute-start | bytes 3145736 | tf_op jit(solution)/shard_map/ppermute | solution.py:11
  389.3 7.3 %scatter_custom_fusion = f32[1024,256]{1,0:T(8,128)S(1)} fusion(s32[1024]{0:T(1024)S(1)} %get-tuple-element.85, f32[1024,256]{1,0:T(8,128)} %bitcast.104, bf16[1024,256]{1,0:T(8,128)(2,1)S(1)} %copy-done.3, f32[1024]{0:T(1024)S(1)} %divide_multiply_fusion, f32[]{:T(128)} %constant.32.clone.1), kind=kCustom, calls=%fused_computation.29 | custom fusion | flops 1048576 | bytes 2625540 | tf_op jit(solution)/shard_map/scatter-add | solution.py:118
  396.7 2.1 collective-permute-start.4
  398.8 0.2 multiply_reduce_fusion.1
  399.0 33.0 %collective-permute-done.4 = f32[1024]{0:T(1024)S(1)} collective-permute-done((f32[1024]{0:T(1024)S(1)}, f32[1024]{0:T(1024)S(1)}, u32[]{:S(2)}, u32[]{:S(2)}) %collective-permute-start.4) | collective-permute-done | bytes 4128 | tf_op jit(solution)/shard_map/ppermute | solution.py:11
  431.9 5.6 %collective-permute-start.5 = (f32[1024]{0:T(1024)S(1)}, f32[1024]{0:T(1024)S(1)}, u32[]{:S(2)}, u32[]{:S(2)}) collective-permute-start(f32[1024]{0:T(1024)S(1)} %broadcast_select_fusion.6), channel_id=1, source_target_pairs={{0,64},{32,96},{64,0},{96,32},{128,192},{160,224},{192,128},{224,1... | collective-permute-start | bytes 12296 | tf_op jit(solution)/shard_map/ppermute | solution.py:11
  437.6 0.1 broadcast_select_fusion.2
  437.7 3.2 collective-permute-start.3
  440.9 5.0 %collective-permute-start.6 = (f32[1024]{0:T(1024)S(1)}, f32[1024]{0:T(1024)S(1)}, u32[]{:S(2)}, u32[]{:S(2)}) collective-permute-start(f32[1024]{0:T(1024)S(1)} %broadcast_select_fusion.7), channel_id=1, source_target_pairs={{0,128},{32,160},{64,192},{96,224},{128,0},{160,32},{192,64},{224,... | collective-permute-start | bytes 12296 | tf_op jit(solution)/shard_map/ppermute | solution.py:11
  445.9 0.6 sqrt_add_fusion.1
  446.5 3.8 collective-permute-done.6
  450.3 4.2 collective-permute-start.7
  454.5 1.2 divide_subtract_fusion.1
  455.7 10.0 %collective-permute-done.7 = f32[1024]{0:T(1024)S(1)} collective-permute-done((f32[1024]{0:T(1024)S(1)}, f32[1024]{0:T(1024)S(1)}, u32[]{:S(2)}, u32[]{:S(2)}) %collective-permute-start.7) | collective-permute-done | bytes 4128 | tf_op jit(solution)/shard_map/ppermute | solution.py:11
  465.7 0.6 broadcast_select_fusion.9
  466.3 1.1 broadcast_select_fusion.3
  (66 shorter events, 1.1 us)
Async XLA Ops:
  0.6 23.9 %copy-start.13 = (s32[2]{0:T(128)S(1)}, s32[2]{0:T(128)}, u32[]{:S(2)}) copy-start(s32[2]{0:T(128)} %constant.85) | copy-start | bytes 28
  0.6 24.0 %copy-start.12 = (s32[2]{0:T(128)S(1)}, s32[2]{0:T(128)}, u32[]{:S(2)}) copy-start(s32[2]{0:T(128)} %constant.82) | copy-start | bytes 28
  0.7 23.7 %copy-start.7 = (s32[2048,1]{0,1:T(1,128)S(1)}, s32[2048,1]{0,1:T(1,128)}, u32[]{:S(2)}) copy-start(s32[2048,1]{0,1:T(1,128)} %param.20) | copy-start | bytes 24580
  0.7 28.6 %copy-start.8 = (s32[2048]{0:T(1024)S(1)}, s32[2048]{0:T(1024)}, u32[]{:S(2)}) copy-start(s32[2048]{0:T(1024)} %param.21) | copy-start | bytes 24580
  29.2 27.5 %copy-start = (f32[1024,256]{1,0:T(8,128)S(1)}, f32[1024,256]{1,0:T(8,128)}, u32[]{:S(2)}) copy-start(f32[1024,256]{1,0:T(8,128)} %param.15) | copy-start | bytes 3145732
  68.1 6.4 %copy-start.9 = (s32[1024]{0:T(1024)S(1)}, s32[1024]{0:T(1024)}, u32[]{:S(2)}) copy-start(s32[1024]{0:T(1024)} %param.17) | copy-start | bytes 12292
  68.1 62.9 %all-to-all-start.1 = ((bf16[32,144,256]{2,1,0:T(8,128)(2,1)}), bf16[32,144,256]{2,1,0:T(8,128)(2,1)}, u32[]{:S(2)}, u32[]{:S(2)}) async-start(bf16[32,144,256]{2,1,0:T(8,128)(2,1)} %bitcast.103), calls=%async_computation.1 | async-start | bytes 4718592 | tf_op jit(solution)/shard_map/all_to_all | solution.py:71
  166.1 2.8 copy-start.4
  166.1 2.8 copy-start.5
  168.9 1.0 copy-start.2
  170.0 1.7 copy-start.6
  171.7 2.8 copy-start.4
  171.7 2.8 copy-start.5
  174.6 1.0 copy-start.2
  175.6 1.7 copy-start.6
  216.8 62.0 %all-to-all-start.2 = ((bf16[32,144,256]{2,1,0:T(8,128)(2,1)}), bf16[32,144,256]{2,1,0:T(8,128)(2,1)}, u32[]{:S(2)}, u32[]{:S(2)}) async-start(bf16[32,144,256]{2,1,0:T(8,128)(2,1)} %bitcast.102), calls=%async_computation.2 | async-start | bytes 4718592 | tf_op jit(solution)/shard_map/all_to_all | solution.py:112
  221.6 81.2 %copy-start.10 = (f32[1024]{0:T(1024)S(1)}, f32[1024]{0:T(1024)}, u32[]{:S(2)}) copy-start(f32[1024]{0:T(1024)} %param.16) | copy-start | bytes 12292
  302.5 3.9 copy-start.14
  303.0 26.5 %collective-permute-start = (f32[1024,256]{1,0:T(8,128)S(1)}, f32[1024,256]{1,0:T(8,128)S(1)}, u32[]{:S(2)}, u32[]{:S(2)}) collective-permute-start(f32[1024,256]{1,0:T(8,128)S(1)} %divide_subtract_fusion), channel_id=1, source_target_pairs={{0,32},{32,0},{64,96},{96,64},{128,160},{160,128},{192,224},{224,1... | collective-permute-start | bytes 3145736 | tf_op jit(solution)/shard_map/ppermute | solution.py:11
  329.6 59.7 %copy-start.3 = (bf16[1024,256]{1,0:T(8,128)(2,1)S(1)}, bf16[1024,256]{1,0:T(8,128)(2,1)}, u32[]{:S(2)}) copy-start(bf16[1024,256]{1,0:T(8,128)(2,1)} %gather_fusion.2) | copy-start | bytes 1572868
  329.7 51.2 %collective-permute-start.1 = (f32[1024,256]{1,0:T(8,128)S(1)}, f32[1024,256]{1,0:T(8,128)S(1)}, u32[]{:S(2)}, u32[]{:S(2)}) collective-permute-start(f32[1024,256]{1,0:T(8,128)S(1)} %broadcast_select_fusion), channel_id=1, source_target_pairs={{0,64},{32,96},{64,0},{96,32},{128,192},{160,224},{192,128},{224,1... | collective-permute-start | bytes 3145736 | tf_op jit(solution)/shard_map/ppermute | solution.py:11
  381.0 56.6 %collective-permute-start.2 = (f32[1024,256]{1,0:T(8,128)S(1)}, f32[1024,256]{1,0:T(8,128)}, u32[]{:S(2)}, u32[]{:S(2)}) collective-permute-start(f32[1024,256]{1,0:T(8,128)S(1)} %broadcast_select_fusion.1), channel_id=1, source_target_pairs={{0,128},{32,160},{64,192},{96,224},{128,0},{160,32},{192,64},{224,... | collective-permute-start | bytes 3145736 | tf_op jit(solution)/shard_map/ppermute | solution.py:11
  396.7 49.2 %copy-start.11 = (f32[1024]{0:T(1024)S(1)}, f32[1024]{0:T(1024)}, u32[]{:S(2)}) copy-start(f32[1024]{0:T(1024)} %param.14) | copy-start | bytes 12292
  396.7 57.8 %copy-start.1 = (f32[1024,256]{1,0:T(8,128)S(1)}, f32[1024,256]{1,0:T(8,128)}, u32[]{:S(2)}) copy-start(f32[1024,256]{1,0:T(8,128)} %param.13) | copy-start | bytes 3145732
  396.7 35.2 %collective-permute-start.4 = (f32[1024]{0:T(1024)S(1)}, f32[1024]{0:T(1024)S(1)}, u32[]{:S(2)}, u32[]{:S(2)}) collective-permute-start(f32[1024]{0:T(1024)S(1)} %get-tuple-element.73), channel_id=1, source_target_pairs={{0,32},{32,0},{64,96},{96,64},{128,160},{160,128},{192,224},{224,1... | collective-permute-start | bytes 12296 | tf_op jit(solution)/shard_map/ppermute | solution.py:11
  431.9 8.9 %collective-permute-start.5 = (f32[1024]{0:T(1024)S(1)}, f32[1024]{0:T(1024)S(1)}, u32[]{:S(2)}, u32[]{:S(2)}) collective-permute-start(f32[1024]{0:T(1024)S(1)} %broadcast_select_fusion.6), channel_id=1, source_target_pairs={{0,64},{32,96},{64,0},{96,32},{128,192},{160,224},{192,128},{224,1... | collective-permute-start | bytes 12296 | tf_op jit(solution)/shard_map/ppermute | solution.py:11
  437.7 28.6 %collective-permute-start.3 = (f32[1024,256]{1,0:T(8,128)S(1)}, f32[1024,256]{1,0:T(8,128)S(1)}, u32[]{:S(2)}, u32[]{:S(2)}) collective-permute-start(f32[1024,256]{1,0:T(8,128)S(1)} %broadcast_select_fusion.2), channel_id=1, source_target_pairs={{0,256},{32,288},{64,320},{96,352},{128,384},{160,416},{192,448},{... | collective-permute-start | bytes 3145736 | tf_op jit(solution)/shard_map/ppermute | solution.py:11
  440.9 9.4 %collective-permute-start.6 = (f32[1024]{0:T(1024)S(1)}, f32[1024]{0:T(1024)S(1)}, u32[]{:S(2)}, u32[]{:S(2)}) collective-permute-start(f32[1024]{0:T(1024)S(1)} %broadcast_select_fusion.7), channel_id=1, source_target_pairs={{0,128},{32,160},{64,192},{96,224},{128,0},{160,32},{192,64},{224,... | collective-permute-start | bytes 12296 | tf_op jit(solution)/shard_map/ppermute | solution.py:11
  450.3 15.4 %collective-permute-start.7 = (f32[1024]{0:T(1024)S(1)}, f32[1024]{0:T(1024)S(1)}, u32[]{:S(2)}, u32[]{:S(2)}) collective-permute-start(f32[1024]{0:T(1024)S(1)} %broadcast_select_fusion.8), channel_id=1, source_target_pairs={{0,256},{32,288},{64,320},{96,352},{128,384},{160,416},{192,448},{... | collective-permute-start | bytes 12296 | tf_op jit(solution)/shard_map/ppermute | solution.py:11
where the time goes:
time: 469 us; the launch traced here: 467 us
  waiting for transfers between devices  224 us (48%)
  local copies, waits for them, and re-layouts  84.2 us (18%)
  other arithmetic  80.8 us (17%)
  starting transfers between devices  47 us (10%)
  blocking collectives  19.1 us (4%)
  matrix products  10.4 us (2%)
    ppermute x8, waiting for transfers between devices, from_partner(): lax.ppermute(shard, axis, [(i, i ^ 1 << stride) for i in range(lax.axis_s...  116 us
    all_to_all x1, waiting for transfers between devices, per_device(): lax.all_to_all(grad_buffer, 'shard', split_axis=0, concat_axis=0, tiled=T...  57 us
    all_to_all x1, waiting for transfers between devices, per_device(): lax.all_to_all(looked_up, 'shard', split_axis=0, concat_axis=0, tiled=True)  50.7 us
    ppermute x8, starting transfers between devices, from_partner(): lax.ppermute(shard, axis, [(i, i ^ 1 << stride) for i in range(lax.axis_s...  36.6 us
    gather x1, local copies, waits for them, and re-layouts, per_device(): negatives = fetched[neg_owner, neg_place]  35 us
    scatter-add x1, other arithmetic, per_device(): dest_grad = jnp.zeros(dest_slab.shape, jnp.float32).at[asked_rows.reshape...  23.7 us
    unnamed x9, other arithmetic  22 us
    all_to_all x1, blocking collectives, per_device(): lax.all_to_all(request, 'shard', split_axis=0, concat_axis=0, tiled=True)  19.1 us
  transfers between devices with their start and end apart: 10, of which 7 were waited for; matrix products, arithmetic and copies ran while one was open for 3% of the time, Pallas kernels for 0%

commit v1 on v0

v1 whole, which is shorter than its diff:
```python
import functools

import jax
import jax.numpy as jnp
from jax import lax
from jax.experimental import pallas as pl
from jax.experimental.pallas import tpu as pltpu
from jax.sharding import PartitionSpec as P

learn_rate = 0.1
epsilon = 1e-06
PLANE = 4
F32, BF16 = jnp.float32, jnp.bfloat16


def sigmoid(x):
    return 0.5 + 0.5 * jnp.tanh(0.5 * x)


def dot(a, b, ca=1, cb=0):
    return lax.dot_general(a, b, (((ca,), (cb,)), ((), ())), preferred_element_type=F32)


def iota(shape, dim):
    return lax.broadcasted_iota(jnp.int32, shape, dim).astype(F32)


def ones_where(mask):
    return jnp.where(mask, 1.0, 0.0).astype(BF16)


def offset_of(k, planes):
    i = k % planes
    size = i // 2 + 1
    dz = jnp.where(i == planes - 1, 0, size * (1 - 2 * (i % 2)))
    return dz, PLANE - 1 - k // planes


def partner(me, k, planes, sign):
    dz, dw = offset_of(k, planes)
    z = (me // PLANE + sign * dz + planes) % planes
    return z * PLANE + (me % PLANE + sign * dw + PLANE) % PLANE


def running_place(onehot):
    owners, n = onehot.shape
    width = 256
    upto = ones_where(iota((width, width), 0) <= iota((width, width), 1))
    carry = jnp.zeros((owners, 1), F32)
    parts = []
    for start in range(0, n, width):
        piece = onehot[:, start : start + width]
        count = dot(piece, upto) + carry
        carry = count[:, width - 1 : width]
        parts.append(jnp.sum(count * piece.astype(F32), axis=0, keepdims=True) - 1.0)
    return jnp.concatenate(parts, axis=1)


def step_kernel(
    shards,
    edge_slots,
    neg_weight,
    dest_ref,
    source_ref,
    src_rows_ref,
    edge_owner_ref,
    edge_rows_ref,
    neg_owner_ref,
    neg_rows_ref,
    live_ref,
    dest_grad_ref,
    source_sum_ref,
    table,
    src,
    src_t,
    src_hot,
    place,
    ask,
    asked,
    send_rows,
    got_rows,
    send_grads,
    got_grads,
    weights,
    chosen,
    coef_hi,
    coef_lo,
    grad_t,
    ask_send,
    ask_recv,
    row_send,
    row_recv,
    grad_send,
    grad_recv,
):
    bucket = lax.axis_index("bucket")
    me = lax.axis_index("shard")
    planes = shards // PLANE
    edges = src_rows_ref.shape[1]
    rows, features = dest_ref.shape
    slots = send_rows.shape[1]
    wide = ask.shape[2]
    mesh_id = pl.DeviceIdType.MESH

    barrier = pltpu.get_barrier_semaphore()

    def greet(k, carry):
        pl.semaphore_signal(
            barrier, inc=1, device_id=(bucket, partner(me, k, planes, 1)), device_id_type=mesh_id
        )
        return carry

    lax.fori_loop(0, shards - 1, greet, 0)

    edge_owner = edge_owner_ref[...].astype(F32)
    neg_owner = neg_owner_ref[...].astype(F32)
    negs = neg_owner.shape[1]
    edge_hot = ones_where(iota((shards, edges), 0) == edge_owner)
    neg_hot = ones_where(iota((shards, negs), 0) == neg_owner)
    edge_place = running_place(edge_hot)
    neg_place = running_place(neg_hot)
    place[...] = jnp.where(live_ref[...] > 0.0, edge_place, -1.0)

    def asked_ids(hot, rows_ref, slot_row):
        row = rows_ref[...]
        high = (row // 32).astype(F32).astype(BF16)
        low = (row % 32).astype(F32).astype(BF16)
        left = jnp.concatenate([hot * high, hot * low, hot], axis=0)
        at = ones_where(iota((wide, hot.shape[1]), 0) == slot_row)
        return dot(left, at, 1, 1)

    found = asked_ids(edge_hot, edge_rows_ref, edge_place) + asked_ids(
        neg_hot, neg_rows_ref, neg_place + float(edge_slots)
    )
    ids = found[:shards] * 32.0 + found[shards : 2 * shards] + found[2 * shards :] - 1.0
    for owner in range(shards):
        ask[owner] = ids[owner : owner + 1, :]
    asked[me] = ask[me]

    pl.semaphore_wait(barrier, shards - 1)

    def ask_copy(to, frm):
        return pltpu.make_async_remote_copy(
            src_ref=ask.at[to],
            dst_ref=asked.at[frm],
            send_sem=ask_send.at[to],
            recv_sem=ask_recv.at[frm],
            device_id=(bucket, to),
            device_id_type=mesh_id,
        )

    def row_copy(to, frm):
        return pltpu.make_async_remote_copy(
            src_ref=send_rows.at[to],
            dst_ref=got_rows.at[frm],
            send_sem=row_send.at[to],
            recv_sem=row_recv.at[frm],
            device_id=(bucket, to),
            device_id_type=mesh_id,
        )

    def grad_copy(to, frm):
        return pltpu.make_async_remote_copy(
            src_ref=send_grads.at[to],
            dst_ref=got_grads.at[frm],
            send_sem=grad_send.at[to],
            recv_sem=grad_recv.at[frm],
            device_id=(bucket, to),
            device_id_type=mesh_id,
        )

    def start_ask(k, carry):
        ask_copy(partner(me, k, planes, 1), me).start()
        return carry

    lax.fori_loop(0, shards - 1, start_ask, 0)

    table[...] = dest_ref[...].astype(BF16)
    src_hot[...] = ones_where(iota((rows, edges), 0) == src_rows_ref[...].astype(F32))
    source_t = source_ref[...].T.astype(BF16)
    picked_t = dot(source_t, src_hot[...])
    src_t[...] = picked_t.astype(BF16)
    src[...] = picked_t.T.astype(BF16)
    grad_t[...] = jnp.zeros_like(grad_t)

    def look_up(who):
        line = asked[who]
        column = jnp.sum(
            jnp.where(iota((slots, wide), 0) == iota((slots, wide), 1), line, 0.0),
            axis=1,
            keepdims=True,
        )
        hot = ones_where(column == iota((slots, rows), 1))
        return dot(hot, table[...]).astype(BF16)

    def serve(k, carry):
        who = partner(me, k, planes, -1)
        ask_copy(who, who).wait_recv()
        send_rows[who] = look_up(who)
        row_copy(who, me).start()
        return carry

    lax.fori_loop(0, shards - 1, serve, 0)
    got_rows[me] = look_up(me)

    def score(who):
        fetched = got_rows[who]
        targets = fetched[:edge_slots].astype(F32)
        scores = dot(fetched[edge_slots:], src_t[...])
        weight = (live_ref[...] * neg_weight * sigmoid(scores)).astype(BF16)
        weights[who] = weight
        slot_row = jnp.where(edge_owner_ref[...] == who, place[...], -1.0)
        pick = ones_where(iota((edge_slots, edges), 0) == slot_row)
        chosen[who] = pick
        mixed = dot(jnp.concatenate([pick, weight], axis=0), src[...])
        sources = mixed[:edge_slots]
        positive = jnp.sum(sources * targets, axis=1, keepdims=True)
        coef = -sigmoid(-positive)
        part = coef * targets
        high = part.astype(BF16)
        coef_hi[who] = high
        coef_lo[who] = (part - high.astype(F32)).astype(BF16)
        return jnp.concatenate([coef * sources, mixed[edge_slots:]], axis=0).astype(BF16)

    got_grads[me] = score(me)

    def answer(k, carry):
        who = partner(me, k, planes, -1)
        row_copy(who, who).wait_recv()
        send_grads[who] = score(who)
        grad_copy(who, me).start()
        return carry

    lax.fori_loop(0, shards - 1, answer, 0)

    def source_part(who, carry):
        left = jnp.concatenate([got_rows[who][edge_slots:], coef_hi[who], coef_lo[who]], axis=0)
        right = jnp.concatenate([weights[who], chosen[who], chosen[who]], axis=0)
        grad_t[...] += dot(left, right, 0, 0)
        return carry

    lax.fori_loop(0, shards, source_part, 0)
    source_grad = grad_t[...].T
    high = source_grad.astype(BF16)
    low = (source_grad - high.astype(F32)).astype(BF16)
    source_sum_ref[...] = dot(src_hot[...], high) + dot(src_hot[...], low)

    def collect(who):
        hot = ones_where(iota((rows, slots), 0) == asked[who][:, :slots])
        return dot(hot, got_grads[who])

    dest_grad_ref[...] = collect(me)

    def gather_grads(k, carry):
        who = partner(me, k, planes, -1)
        grad_copy(who, who).wait_recv()
        dest_grad_ref[...] += collect(who)
        return carry

    lax.fori_loop(0, shards - 1, gather_grads, 0)

    def finish(k, carry):
        to = partner(me, k, planes, 1)
        ask_copy(to, me).wait_send()
        row_copy(to, me).wait_send()
        grad_copy(to, me).wait_send()
        return carry

    lax.fori_loop(0, shards - 1, finish, 0)


def gradients(dest_slab, source_slab, source_rows, edge_owner, edge_rows, neg_owner, neg_rows, live):
    shards = lax.axis_size("shard")
    edges = source_rows.shape[0]
    negs = neg_rows.shape[0]
    rows, features = dest_slab.shape
    edge_slots = 3 * edges // (2 * shards)
    neg_slots = 3 * negs // (2 * shards)
    slots = edge_slots + neg_slots
    wide = -(-slots // 128) * 128
    vmem = pl.BlockSpec(memory_space=pltpu.VMEM)
    dma = pltpu.SemaphoreType.DMA
    return pl.pallas_call(
        functools.partial(step_kernel, shards, edge_slots, negs ** (-0.5)),
        out_shape=(
            jax.ShapeDtypeStruct((rows, features), F32),
            jax.ShapeDtypeStruct((rows, features), F32),
        ),
        in_specs=[vmem] * 8,
        out_specs=(vmem, vmem),
        scratch_shapes=[
            pltpu.VMEM((rows, features), BF16),
            pltpu.VMEM((edges, features), BF16),
            pltpu.VMEM((features, edges), BF16),
            pltpu.VMEM((rows, edges), BF16),
            pltpu.VMEM((1, edges), F32),
            pltpu.VMEM((shards, 1, wide), F32),
            pltpu.VMEM((shards, 1, wide), F32),
            pltpu.VMEM((shards, slots, features), BF16),
            pltpu.VMEM((shards, slots, features), BF16),
            pltpu.VMEM((shards, slots, features), BF16),
            pltpu.VMEM((shards, slots, features), BF16),
            pltpu.VMEM((shards, neg_slots, edges), BF16),
            pltpu.VMEM((shards, edge_slots, edges), BF16),
            pltpu.VMEM((shards, edge_slots, features), BF16),
            pltpu.VMEM((shards, edge_slots, features), BF16),
            pltpu.VMEM((features, edges), F32),
            dma((shards,)),
            dma((shards,)),
            dma((shards,)),
            dma((shards,)),
            dma((shards,)),
            dma((shards,)),
        ],
        compiler_params=pltpu.CompilerParams(
            collective_id=0, has_side_effects=True, vmem_limit_bytes=56 << 20
        ),
        name="edge_step",
    )(dest_slab, source_slab, source_rows[None], edge_owner[None], edge_rows[None], neg_owner[None], neg_rows[None], live[None])


def adagrad_rows(table_rows, row_state, row_grad):
    fresh_state = row_state + jnp.mean(row_grad * row_grad, axis=1)
    return (
        table_rows - learn_rate * row_grad / (jnp.sqrt(fresh_state)[:, None] + epsilon),
        fresh_state,
    )


def carry_over(table_rows, row_state, matching):
    size = lax.axis_size("bucket")
    largest = jnp.maximum(jnp.max(jnp.abs(table_rows), axis=1), 1e-30)
    coded = jnp.round(table_rows * (32767.0 / largest)[:, None]).astype(jnp.int16)
    beside = jnp.stack([largest, row_state])

    def exchange(mask):
        pairs = [(i, i ^ mask) for i in range(size)]
        return lambda a, b: (lax.ppermute(a, "bucket", pairs), lax.ppermute(b, "bucket", pairs))

    coded, beside = lax.switch(
        matching[0] - 1, [exchange(mask) for mask in range(1, size)], coded, beside
    )
    return coded.astype(F32) * (beside[0] * (1.0 / 32767.0))[:, None], beside[1]


def per_device(
    source_slab,
    source_state,
    dest_slab,
    dest_state,
    source_rows,
    target_owner,
    target_rows,
    negative_owner,
    negative_rows,
    edge_count,
    matching,
):
    edges = source_rows.shape[0]
    live = (jnp.arange(edges, dtype=jnp.int32) < edge_count[0]).astype(F32)
    dest_grad, source_sum = gradients(
        dest_slab,
        source_slab,
        source_rows,
        target_owner[:, 0],
        target_rows,
        negative_owner[:, 0],
        negative_rows,
        live,
    )
    new_dest, new_dest_state = adagrad_rows(dest_slab, dest_state, dest_grad)
    incoming_rows, incoming_state = carry_over(new_dest, new_dest_state, matching)
    new_source, new_source_state = adagrad_rows(source_slab, source_state, source_sum)
    return (new_source, new_source_state, incoming_rows, incoming_state)


def solution(mesh):
    both = ("bucket", "shard")
    in_specs = (
        P(both, None),
        P(both),
        P(both, None),
        P(both),
        P(both),
        P(both, None),
        P(both),
        P(both, None),
        P(both),
        P(both),
        P(),
    )
    out_specs = (P(both, None), P(both), P(both, None), P(both))
    return jax.shard_map(
        per_device, mesh=mesh, in_specs=in_specs, out_specs=out_specs, check_vma=False
    )
```

time: 469 us -> 171 us (0.36)
  waiting for transfers between devices: 224 us -> 22.2 us
  Pallas kernels: 0 us -> 124 us
  local copies, waits for them, and re-layouts: 84.2 us -> 3.14 us
  other arithmetic: 80.8 us -> 9.6 us
  starting transfers between devices: 47 us -> 9.46 us
  blocking collectives: 19.1 us -> 0 us
  matrix products: 10.4 us -> 0 us
    pallas_call x0 -> x1, Pallas kernels: none -> 124 us  [gradients(): pl.pallas_call(functools.partial(step_kernel, shards, edge_slots, negs **...]
    all_to_all x2 -> x0, waiting for transfers between devices: 108 us -> none  [the longest x1 57 us: per_device(): lax.all_to_all(grad_buffer, 'shard', split_axis=0, concat_axis=0, tiled=T...]
    ppermute x8 -> x2, waiting for transfers between devices: 116 us -> 22.2 us  [the longest x1 22.2 us: exchange(): lax.ppermute(b, 'bucket', pairs)]
    gather x4 -> x0, local copies, waits for them, and re-layouts: 70 us -> none  [the longest x1 35 us: per_device(): negatives = fetched[neg_owner, neg_place]]
    scatter-add x2 -> x0, other arithmetic: 31 us -> none  [the longest x1 23.7 us: per_device(): dest_grad = jnp.zeros(dest_slab.shape, jnp.float32).at[asked_rows.reshape...]
    ppermute x8 -> x2, starting transfers between devices: 36.6 us -> 9.46 us  [the longest x1 6.13 us: exchange(): lax.ppermute(a, 'bucket', pairs)]
    unnamed x9 -> x0, other arithmetic: 22 us -> none
    all_to_all x1 -> x0, blocking collectives: 19.1 us -> none  [per_device(): lax.all_to_all(request, 'shard', split_axis=0, concat_axis=0, tiled=True)]
  transfers between devices with their start and end apart: 10 -> 2, of which waited for: 7 -> 1; matrix products, arithmetic and copies ran while one was open for 3% -> 1% of each run, Pallas kernels for 0% -> 0%
where the time goes in v1:
time: 171 us; the launch traced here: 170 us
  Pallas kernels  124 us (73%)
  waiting for transfers between devices  22.2 us (13%)
  other arithmetic  9.6 us (6%)
  starting transfers between devices  9.46 us (6%)
  local copies, waits for them, and re-layouts  3.14 us (2%)
    pallas_call x1, Pallas kernels, gradients(): pl.pallas_call(functools.partial(step_kernel, shards, edge_slots, negs **...  124 us
    ppermute x1, waiting for transfers between devices, exchange(): lax.ppermute(b, 'bucket', pairs)  22.2 us
    ppermute x1, starting transfers between devices, exchange(): lax.ppermute(a, 'bucket', pairs)  6.13 us
  transfers between devices with their start and end apart: 2, of which 1 were waited for; matrix products, arithmetic and copies ran while one was open for 1% of the time, Pallas kernels for 0%

profile of v1, /device:TPU:6, one launch (start us, length us, event | category | flops | bytes accessed | tf_op | source)
XLA Modules:
  0.0 169.6 jit_solution(12547593015946108773)
XLA Ops:
  1.3 0.6 compare_convert_fusion.live_ref
  1.9 0.0 copy-start.33
  1.9 123.7 %edge_step.1 = (f32[1024,256]{1,0:T(8,128)}, f32[1024,256]{1,0:T(8,128)}) custom-call(f32[1024,256]{1,0:T(8,128)} %dest_ref.1, f32[1024,256]{1,0:T(8,128)} %source_ref.1, s32[1,1024]{1,0:T(1,128)} %bitcast.62, s32[1,1024]{1,0:T(1,128)} %bitcast.63, s32[1,1024]{1,0:T(1,128)} %bitcast.64, s32[1,2048]{1,0:T(1,128)} %bitcast.60, s32[1,2048]{1,0:T(1,128)} %bitcast.61, ...), custom_call_target="tpu_custom_call" | custom-call | tf_op jit(solution)/shard_map/edge_step/pallas_call | solution.py:283
  125.6 0.0 copy-start
  125.6 0.0 copy-start.1
  125.6 1.6 multiply_reduce_fusion
  127.2 0.0 copy-done.33
  127.2 0.0 copy-start.34
  127.2 1.4 multiply_reduce_fusion.1
  128.7 0.0 copy-done.34
  128.7 0.6 sqrt_add_fusion.1
  129.3 0.0 copy-done
  129.3 0.0 copy-done.1
  129.3 2.9 %abs_reduce_fusion = (f32[1024]{0:T(1024)S(1)}, f32[1024,256]{1,0:T(8,128)S(1)}, f32[1024,256]{1,0:T(8,128)}) fusion(f32[1024,256]{1,0:T(8,128)S(1)} %copy-done, f32[1024]{0:T(1024)S(1)} %get-tuple-element.134, f32[1024,256]{1,0:T(8,128)} %get-tuple-element.120, f32[1024,256]{1,0:T(8,128)S(1)} %copy-done.1, f32[1024]{0:T(1024)S(1)} %get-tuple-element.136, ...), kind=kLoop, calls=%fused_computation.2 | loop fusion | flops 2096128 | bytes 6303744 | tf_op jit(solution)/shard_map/reduce_max | solution.py:332
  132.2 0.2 round-nearest-even_convert_fusion
  132.4 0.0 copy-start.35
  132.5 0.6 copy-done.35
  133.1 33.6 %conditional.4 = (f32[2,1024]{1,0:T(2,128)}, f32[1,1024]{1,0:T(1,128)}, f32[1,1024]{1,0:T(1,128)}, f32[1024,1]{0,1:T(1,128)S(1)}, f32[1024]{0:T(1024)S(1)}, /*index=5*/s16[1024,256]{1,0:T(8,128)(2,1)}) conditional(s32[]{:T(128)} %bitcast.36, (f32[2,1024]{1,0:T(2,128)S(1)}, s16[1024,256]{1,0:T(8,128)(2,1)S(1)}) %tuple.145, ...), branch_computations={%region_3.4_spmd, %region_4.5_spmd, %region_5.6_spmd, %region_6.7_... | conditional | bytes 2212024
  133.2 6.1 %collective-permute-start.29 = (s16[1024,256]{1,0:T(8,128)(2,1)S(1)}, s16[1024,256]{1,0:T(8,128)(2,1)}, u32[]{:S(2)}, u32[]{:S(2)}) collective-permute-start(s16[1024,256]{1,0:T(8,128)(2,1)S(1)} %get-tuple-element.109), channel_id=1, source_target_pairs={{0,480},{32,448},{64,416},{96,384},{128,352},{160,320},{192,288},{... | collective-permute-start | bytes 1572872 | tf_op jit(solution)/shard_map/cond/branch_14_fun/ppermute | solution.py:338
  139.3 3.3 %collective-permute-start.28 = (f32[2,1024]{1,0:T(2,128)S(1)}, f32[2,1024]{1,0:T(2,128)S(1)}, u32[]{:S(2)}, u32[]{:S(2)}) collective-permute-start(f32[2,1024]{1,0:T(2,128)S(1)} %get-tuple-element.108), channel_id=1, source_target_pairs={{0,480},{32,448},{64,416},{96,384},{128,352},{160,320},{192,288},{... | collective-permute-start | bytes 24584 | tf_op jit(solution)/shard_map/cond/branch_14_fun/ppermute | solution.py:338
  142.7 22.2 %collective-permute-done.28 = f32[2,1024]{1,0:T(2,128)S(1)} collective-permute-done((f32[2,1024]{1,0:T(2,128)S(1)}, f32[2,1024]{1,0:T(2,128)S(1)}, u32[]{:S(2)}, u32[]{:S(2)}) %collective-permute-start.28) | collective-permute-done | bytes 8224 | tf_op jit(solution)/shard_map/cond/branch_14_fun/ppermute | solution.py:338
  164.9 0.0 copy-start.16
  164.9 0.6 fusion.14
  165.5 0.0 copy-done.16
  165.5 0.0 copy-start.31
  165.5 0.6 copy-done.31
  166.1 0.7 copy.103
  166.7 0.0 collective-permute-done.29
  166.7 0.0 copy-start.32
  166.8 0.6 copy-done.32
  167.3 2.2 %convert_multiply_fusion = f32[1024,256]{1,0:T(8,128)} fusion(s16[1024,256]{1,0:T(8,128)(2,1)} %get-tuple-element.131, f32[1024]{0:T(1024)S(1)} %bitcast.57), kind=kLoop, calls=%fused_computation | loop fusion | flops 524288 | bytes 1576960 | tf_op jit(solution)/shard_map/mul | solution.py:343
  (5 shorter events, 0.0 us)
Async XLA Ops:
  1.9 125.3 %copy-start.33 = (f32[1024]{0:T(1024)S(1)}, f32[1024]{0:T(1024)}, u32[]{:S(2)}) copy-start(f32[1024]{0:T(1024)} %param.29) | copy-start | bytes 12292
  125.6 3.7 %copy-start = (f32[1024,256]{1,0:T(8,128)S(1)}, f32[1024,256]{1,0:T(8,128)}, u32[]{:S(2)}) copy-start(f32[1024,256]{1,0:T(8,128)} %dest_ref.1) | copy-start | bytes 3145732
  125.6 3.7 %copy-start.1 = (f32[1024,256]{1,0:T(8,128)S(1)}, f32[1024,256]{1,0:T(8,128)}, u32[]{:S(2)}) copy-start(f32[1024,256]{1,0:T(8,128)} %source_ref.1) | copy-start | bytes 3145732
  127.2 1.5 copy-start.34
  132.4 0.7 copy-start.35
  133.2 33.5 %collective-permute-start.29 = (s16[1024,256]{1,0:T(8,128)(2,1)S(1)}, s16[1024,256]{1,0:T(8,128)(2,1)}, u32[]{:S(2)}, u32[]{:S(2)}) collective-permute-start(s16[1024,256]{1,0:T(8,128)(2,1)S(1)} %get-tuple-element.109), channel_id=1, source_target_pairs={{0,480},{32,448},{64,416},{96,384},{128,352},{160,320},{192,288},{... | collective-permute-start | bytes 1572872 | tf_op jit(solution)/shard_map/cond/branch_14_fun/ppermute | solution.py:338
  139.3 25.5 %collective-permute-start.28 = (f32[2,1024]{1,0:T(2,128)S(1)}, f32[2,1024]{1,0:T(2,128)S(1)}, u32[]{:S(2)}, u32[]{:S(2)}) collective-permute-start(f32[2,1024]{1,0:T(2,128)S(1)} %get-tuple-element.108), channel_id=1, source_target_pairs={{0,480},{32,448},{64,416},{96,384},{128,352},{160,320},{192,288},{... | collective-permute-start | bytes 24584 | tf_op jit(solution)/shard_map/cond/branch_14_fun/ppermute | solution.py:338
  164.9 0.6 copy-start.16
  165.5 0.6 copy-start.31
  166.7 0.6 copy-start.32

commit v2 on v1

v2 whole, which is shorter than its diff:
```python
import functools

import jax
import jax.numpy as jnp
from jax import lax
from jax.experimental import pallas as pl
from jax.experimental.pallas import tpu as pltpu
from jax.sharding import PartitionSpec as P

learn_rate = 0.1
epsilon = 1e-06
CODE = 32767.0
PLANE = 4
F32, BF16 = jnp.float32, jnp.bfloat16


def sigmoid(x):
    return 0.5 + 0.5 * jnp.tanh(0.5 * x)


def dot(a, b, ca=1, cb=0):
    return lax.dot_general(a, b, (((ca,), (cb,)), ((), ())), preferred_element_type=F32)


def iota(shape, dim):
    return lax.broadcasted_iota(jnp.int32, shape, dim).astype(F32)


def ones_where(mask):
    return jnp.where(mask, 1.0, 0.0).astype(BF16)


def around(i):
    return (i + 1) // 2 * (2 * (i % 2) - 1)


def partner(me, k, planes):
    z = (me // PLANE + around(k // PLANE) + planes) % planes
    return z * PLANE + (me % PLANE + k) % PLANE


def column(row):
    n = row.shape[1]
    return jnp.broadcast_to(row, (n, n)).T[:, :1]


def row_of(col):
    n = col.shape[0]
    return jnp.broadcast_to(col, (n, n)).T[:1, :]


def running_place(onehot):
    owners, n = onehot.shape
    width = 256
    upto = ones_where(iota((width, width), 0) <= iota((width, width), 1))
    carry = jnp.zeros((owners, 1), F32)
    parts = []
    for start in range(0, n, width):
        piece = onehot[:, start : start + width]
        count = dot(piece, upto) + carry
        carry = count[:, width - 1 : width]
        parts.append(jnp.sum(count * piece.astype(F32), axis=0, keepdims=True) - 1.0)
    return jnp.concatenate(parts, axis=1)


def step_kernel(
    edge_slots,
    neg_weight,
    dest_ref,
    dest_state_ref,
    source_ref,
    source_state_ref,
    src_rows_ref,
    edge_owner_ref,
    edge_rows_ref,
    neg_owner_ref,
    neg_rows_ref,
    live_ref,
    new_source_ref,
    new_source_state_ref,
    coded_ref,
    beside_ref,
    tables,
    src,
    src_t,
    src_hot,
    place,
    ask,
    asked,
    mate_ask,
    mate_asked,
    send_rows,
    got_rows,
    send_grads,
    got_grads,
    weights,
    chosen,
    coef_hi,
    coef_lo,
    grad_t,
    dest_grad,
    ask_send,
    ask_recv,
    mate_send,
    mate_recv,
    table_send,
    table_recv,
    row_send,
    row_recv,
    grad_send,
    grad_recv,
):
    bucket = lax.axis_index("bucket")
    me = lax.axis_index("shard")
    z, w = me // PLANE, me % PLANE
    planes = tables.shape[0]
    half = planes // 2
    shards = planes * PLANE
    edges = src_rows_ref.shape[1]
    rows, features = dest_ref.shape
    chunk = rows // 2
    slots = got_rows.shape[1]
    wide = ask.shape[2]

    def copy_to(to, src_ref, dst_ref, send_sem, recv_sem):
        return pltpu.make_async_remote_copy(
            src_ref=src_ref,
            dst_ref=dst_ref,
            send_sem=send_sem,
            recv_sem=recv_sem,
            device_id=(bucket, to),
            device_id_type=pl.DeviceIdType.MESH,
        )

    def ask_copy(to, frm):
        return copy_to(to, ask.at[to], asked.at[frm], ask_send.at[to], ask_recv.at[frm])

    def mate_copy(to, frm):
        return copy_to(
            z * PLANE + to, mate_ask.at[to], mate_asked.at[frm], mate_send.at[to], mate_recv.at[frm]
        )

    def table_copy(way, step, part):
        frm = (z - way * step + planes) % planes
        at = tables.at[frm, pl.ds(part * chunk, chunk)]
        return copy_to(
            (z + way + planes) % planes * PLANE + w,
            at,
            at,
            table_send.at[(way + 1) // 2, step, part],
            table_recv.at[frm, part],
        )

    def row_copy(to, frm, plane):
        return copy_to(
            z * PLANE + to,
            send_rows.at[plane, to],
            got_rows.at[plane * PLANE + frm],
            row_send.at[plane, to],
            row_recv.at[plane * PLANE + frm],
        )

    def grad_copy(to, frm):
        return copy_to(to, send_grads.at[to], got_grads.at[frm], grad_send.at[to], grad_recv.at[frm])

    barrier = pltpu.get_barrier_semaphore()

    def greet(k, carry):
        pl.semaphore_signal(
            barrier,
            inc=1,
            device_id=(bucket, partner(me, k, planes)),
            device_id_type=pl.DeviceIdType.MESH,
        )
        return carry

    lax.fori_loop(1, shards, greet, 0)
    tables[z] = dest_ref[...].astype(BF16)
    pl.semaphore_wait(barrier, shards - 1)

    def parts_of(way, step):
        return (0, 1) if step < half - 1 else ((0,) if way > 0 else (1,))

    def pass_on(step):
        for part in (0, 1):
            for way in (1, -1):
                if part in parts_of(way, step):
                    table_copy(way, step, part).start()

    pass_on(0)

    edge_owner = edge_owner_ref[...].astype(F32)
    neg_owner = neg_owner_ref[...].astype(F32)
    negs = neg_owner.shape[1]
    edge_hot = ones_where(iota((shards, edges), 0) == edge_owner)
    neg_hot = ones_where(iota((shards, negs), 0) == neg_owner)
    edge_place = running_place(edge_hot)
    neg_place = running_place(neg_hot)
    place[...] = jnp.where(live_ref[...] > 0.0, edge_place, -1.0)

    def asked_ids(hot, rows_ref, slot_row):
        row = rows_ref[...]
        high = (row // 32).astype(F32).astype(BF16)
        low = (row % 32).astype(F32).astype(BF16)
        left = jnp.concatenate([hot * high, hot * low, hot], axis=0)
        at = ones_where(iota((wide, hot.shape[1]), 0) == slot_row)
        return dot(left, at, 1, 1)

    found = asked_ids(edge_hot, edge_rows_ref, edge_place) + asked_ids(
        neg_hot, neg_rows_ref, neg_place + float(edge_slots)
    )
    ids = found[:shards] * 32.0 + found[shards : 2 * shards] + found[2 * shards :] - 1.0
    for owner in range(shards):
        line = ids[owner : owner + 1, :]
        ask[owner] = line
        mate_ask[owner % PLANE, owner // PLANE] = line
    asked[me] = ask[me]
    mate_asked[w] = mate_ask[w]
    for k in range(1, PLANE):
        mate_copy((w + k) % PLANE, w).start()

    def start_ask(k, carry):
        ask_copy(partner(me, k, planes), me).start()
        return carry

    lax.fori_loop(1, shards, start_ask, 0)

    src_hot[...] = ones_where(iota((rows, edges), 0) == src_rows_ref[...].astype(F32))
    source_t = source_ref[...].T.astype(BF16)
    picked_t = dot(source_t, src_hot[...])
    src_t[...] = picked_t.astype(BF16)
    src[...] = picked_t.T.astype(BF16)
    grad_t[...] = jnp.zeros_like(grad_t)
    for k in range(1, PLANE):
        mate_copy((w + k) % PLANE, (w + k) % PLANE).wait_recv()

    def serve(plane):
        hots = []
        for k in range(PLANE):
            line = mate_asked[(w + k) % PLANE, plane]
            spread = jnp.where(iota((slots, wide), 0) == iota((slots, wide), 1), line, 0.0)
            at = jnp.sum(spread, axis=1, keepdims=True)
            hots.append(ones_where(at == iota((slots, rows), 1)))
        found = dot(jnp.concatenate(hots, axis=0), tables[plane]).astype(BF16)
        for k in range(1, PLANE):
            to = (w + k) % PLANE
            send_rows[plane, to] = found[k * slots : (k + 1) * slots]
            row_copy(to, w, plane).start()
        got_rows[plane * PLANE + w] = found[:slots]

    def score(who):
        fetched = got_rows[who]
        targets = fetched[:edge_slots].astype(F32)
        scores = dot(fetched[edge_slots:], src_t[...])
        weight = (live_ref[...] * neg_weight * sigmoid(scores)).astype(BF16)
        weights[who] = weight
        slot_row = jnp.where(edge_owner_ref[...] == who, place[...], -1.0)
        pick = ones_where(iota((edge_slots, edges), 0) == slot_row)
        chosen[who] = pick
        mixed = dot(jnp.concatenate([pick, weight], axis=0), src[...])
        sources = mixed[:edge_slots]
        positive = jnp.sum(sources * targets, axis=1, keepdims=True)
        coef = -sigmoid(-positive)
        part = coef * targets
        high = part.astype(BF16)
        coef_hi[who] = high
        coef_lo[who] = (part - high.astype(F32)).astype(BF16)
        return jnp.concatenate([coef * sources, mixed[edge_slots:]], axis=0).astype(BF16)

    def answer(k, carry):
        who = partner(me, k, planes)
        mine = (w + k) % PLANE

        @pl.when(mine != w)
        def _():
            row_copy(w, mine, who // PLANE).wait_recv()

        send_grads[who] = score(who)
        grad_copy(who, me).start()
        return carry

    def serve_next(i, carry):
        serve((z + around(i) + planes) % planes)
        return carry

    def arrive(step):
        for part in (0, 1):
            for way in (1, -1):
                if part in parts_of(way, step - 1):
                    frm = (z - way * step + planes) % planes
                    at = tables.at[frm, pl.ds(part * chunk, chunk)]
                    copy_to(
                        (z - way + planes) % planes * PLANE + w,
                        at,
                        at,
                        table_send.at[0, 0, 0],
                        table_recv.at[frm, part],
                    ).wait_recv()
                    if step < half and part in parts_of(way, step):
                        table_copy(way, step, part).start()

    serve(z)
    for step in range(1, half + 1):
        arrive(step)
        lax.fori_loop(2 * step - 1, min(2 * step + 1, planes), serve_next, 0)
        if step == 1:
            got_grads[me] = score(me)
            lax.fori_loop(1, PLANE, answer, 0)
        else:
            lax.fori_loop((2 * step - 3) * PLANE, (2 * step - 1) * PLANE, answer, 0)
    lax.fori_loop((planes - 1) * PLANE, shards, answer, 0)

    def source_part(who, carry):
        left = jnp.concatenate([got_rows[who][edge_slots:], coef_hi[who], coef_lo[who]], axis=0)
        right = jnp.concatenate([weights[who], chosen[who], chosen[who]], axis=0)
        grad_t[...] += dot(left, right, 0, 0)
        return carry

    lax.fori_loop(0, shards, source_part, 0)
    source_grad = grad_t[...].T
    high = source_grad.astype(BF16)
    low = (source_grad - high.astype(F32)).astype(BF16)
    new_source_ref[...] = dot(src_hot[...], high) + dot(src_hot[...], low)
    block = 128

    def update(grad, table_ref, state_ref, at):
        mean = jnp.sum(grad * grad, axis=1, keepdims=True) * (1.0 / features)
        state = column(state_ref[:, at]) + mean
        return table_ref[at, :] - grad * (learn_rate / (jnp.sqrt(state) + epsilon)), state

    def update_source(i, carry):
        at = pl.ds(pl.multiple_of(i * block, block), block)
        fresh, state = update(new_source_ref[at, :], source_ref, source_state_ref, at)
        new_source_ref[at, :] = fresh
        new_source_state_ref[:, at] = row_of(state)
        return carry

    lax.fori_loop(0, rows // block, update_source, 0)

    def collect(who):
        hot = ones_where(iota((rows, slots), 0) == asked[who][:, :slots])
        return dot(hot, got_grads[who])

    dest_grad[...] = collect(me)

    def gather_grads(k, carry):
        who = partner(me, k, planes)
        ask_copy(who, who).wait_recv()
        grad_copy(who, who).wait_recv()
        dest_grad[...] += collect(who)
        return carry

    lax.fori_loop(1, shards, gather_grads, 0)

    def update_dest(i, carry):
        at = pl.ds(pl.multiple_of(i * block, block), block)
        fresh, state = update(dest_grad[at, :], dest_ref, dest_state_ref, at)
        largest = jnp.maximum(jnp.max(jnp.abs(fresh), axis=1, keepdims=True), 1e-30)
        coded_ref[at, :] = jnp.round(fresh * (CODE / largest)).astype(jnp.int16)
        beside_ref[0:1, at] = row_of(largest)
        beside_ref[1:2, at] = row_of(state)
        return carry

    lax.fori_loop(0, rows // block, update_dest, 0)

    def sent(k, carry):
        to = partner(me, k, planes)
        ask_copy(to, me).wait_send()
        grad_copy(to, me).wait_send()
        return carry

    lax.fori_loop(1, shards, sent, 0)
    for k in range(1, PLANE):
        to = (w + k) % PLANE
        mate_copy(to, w).wait_send()

        def rows_sent(plane, carry):
            row_copy(to, w, plane).wait_send()
            return carry

        lax.fori_loop(0, planes, rows_sent, 0)
    for step in range(half):
        for way in (1, -1):
            for part in parts_of(way, step):
                table_copy(way, step, part).wait_send()


def device_step(
    dest_slab,
    dest_state,
    source_slab,
    source_state,
    source_rows,
    edge_owner,
    edge_rows,
    neg_owner,
    neg_rows,
    live,
):
    shards = lax.axis_size("shard")
    planes = shards // PLANE
    edges = source_rows.shape[0]
    negs = neg_rows.shape[0]
    rows, features = dest_slab.shape
    edge_slots = 3 * edges // (2 * shards)
    neg_slots = 3 * negs // (2 * shards)
    slots = edge_slots + neg_slots
    wide = -(-slots // 128) * 128
    vmem = pl.BlockSpec(memory_space=pltpu.VMEM)
    dma = pltpu.SemaphoreType.DMA
    return pl.pallas_call(
        functools.partial(step_kernel, edge_slots, negs ** (-0.5)),
        out_shape=(
            jax.ShapeDtypeStruct((rows, features), F32),
            jax.ShapeDtypeStruct((1, rows), F32),
            jax.ShapeDtypeStruct((rows, features), jnp.int16),
            jax.ShapeDtypeStruct((2, rows), F32),
        ),
        in_specs=[vmem] * 10,
        out_specs=(vmem,) * 4,
        scratch_shapes=[
            pltpu.VMEM((planes, rows, features), BF16),
            pltpu.VMEM((edges, features), BF16),
            pltpu.VMEM((features, edges), BF16),
            pltpu.VMEM((rows, edges), BF16),
            pltpu.VMEM((1, edges), F32),
            pltpu.VMEM((shards, 1, wide), F32),
            pltpu.VMEM((shards, 1, wide), F32),
            pltpu.VMEM((PLANE, planes, 1, wide), F32),
            pltpu.VMEM((PLANE, planes, 1, wide), F32),
            pltpu.VMEM((planes, PLANE, slots, features), BF16),
            pltpu.VMEM((shards, slots, features), BF16),
            pltpu.VMEM((shards, slots, features), BF16),
            pltpu.VMEM((shards, slots, features), BF16),
            pltpu.VMEM((shards, neg_slots, edges), BF16),
            pltpu.VMEM((shards, edge_slots, edges), BF16),
            pltpu.VMEM((shards, edge_slots, features), BF16),
            pltpu.VMEM((shards, edge_slots, features), BF16),
            pltpu.VMEM((features, edges), F32),
            pltpu.VMEM((rows, features), F32),
            dma((shards,)),
            dma((shards,)),
            dma((PLANE,)),
            dma((PLANE,)),
            dma((2, planes // 2, 2)),
            dma((planes, 2)),
            dma((planes, PLANE)),
            dma((shards,)),
            dma((shards,)),
            dma((shards,)),
        ],
        compiler_params=pltpu.CompilerParams(
            collective_id=0, has_side_effects=True, vmem_limit_bytes=58 << 20
        ),
        name="edge_step",
    )(
        dest_slab,
        dest_state[None],
        source_slab,
        source_state[None],
        source_rows[None],
        edge_owner[None],
        edge_rows[None],
        neg_owner[None],
        neg_rows[None],
        live[None],
    )


def carry_over(coded, beside, matching):
    size = lax.axis_size("bucket")

    def exchange(mask):
        pairs = [(i, i ^ mask) for i in range(size)]
        return lambda a, b: (lax.ppermute(a, "bucket", pairs), lax.ppermute(b, "bucket", pairs))

    coded, beside = lax.switch(
        matching[0] - 1, [exchange(mask) for mask in range(1, size)], coded, beside
    )
    return coded.astype(F32) * (beside[0] * (1.0 / CODE))[:, None], beside[1]


def per_device(
    source_slab,
    source_state,
    dest_slab,
    dest_state,
    source_rows,
    target_owner,
    target_rows,
    negative_owner,
    negative_rows,
    edge_count,
    matching,
):
    edges = source_rows.shape[0]
    live = (jnp.arange(edges, dtype=jnp.int32) < edge_count[0]).astype(F32)
    new_source, new_source_state, coded, beside = device_step(
        dest_slab,
        dest_state,
        source_slab,
        source_state,
        source_rows,
        target_owner[:, 0],
        target_rows,
        negative_owner[:, 0],
        negative_rows,
        live,
    )
    incoming_rows, incoming_state = carry_over(coded, beside, matching)
    return (new_source, new_source_state[0], incoming_rows, incoming_state)


def solution(mesh):
    both = ("bucket", "shard")
    in_specs = (
        P(both, None),
        P(both),
        P(both, None),
        P(both),
        P(both),
        P(both, None),
        P(both),
        P(both, None),
        P(both),
        P(both),
        P(),
    )
    out_specs = (P(both, None), P(both), P(both, None), P(both))
    return jax.shard_map(
        per_device, mesh=mesh, in_specs=in_specs, out_specs=out_specs, check_vma=False
    )
```

time: 171 us -> 153 us (0.89)
  Pallas kernels: 124 us -> 111 us
  other arithmetic: 9.6 us -> 2.82 us
  starting transfers between devices: 9.46 us -> 7.45 us
    pallas_call x1, Pallas kernels: 124 us -> 111 us  [device_step(): pl.pallas_call(functools.partial(step_kernel, edge_slots, negs ** (-0.5))...]
    reduce_sum x2 -> x0, other arithmetic: 3.02 us -> none  [adagrad_rows(): fresh_state = row_state + jnp.mean(row_grad * row_grad, axis=1)]
    reduce_max x1 -> x0, other arithmetic: 2.92 us -> none  [carry_over(): largest = jnp.maximum(jnp.max(jnp.abs(table_rows), axis=1), 1e-30)]
    unnamed x18 -> x16, local copies, waits for them, and re-layouts: 2.54 us -> 4.09 us
where the time goes in v2:
time: 153 us; the launch traced here: 150 us
  Pallas kernels  111 us (73%)
  waiting for transfers between devices  22.2 us (15%)
  starting transfers between devices  7.45 us (5%)
  local copies, waits for them, and re-layouts  4.68 us (3%)
  other arithmetic  2.82 us (2%)
    pallas_call x1, Pallas kernels, device_step(): pl.pallas_call(functools.partial(step_kernel, edge_slots, negs ** (-0.5))...  111 us
    ppermute x1, waiting for transfers between devices, exchange(): lax.ppermute(b, 'bucket', pairs)  22.2 us
    ppermute x1, starting transfers between devices, exchange(): lax.ppermute(a, 'bucket', pairs)  5.53 us
    unnamed x16, local copies, waits for them, and re-layouts  4.09 us
  transfers between devices with their start and end apart: 2, of which 1 were waited for; matrix products, arithmetic and copies ran while one was open for 1% of the time, Pallas kernels for 0%

profile of v2, /device:TPU:6, one launch (start us, length us, event | category | flops | bytes accessed | tf_op | source)
XLA Modules:
  0.0 150.0 jit_solution(14542620952984996113)
XLA Ops:
  1.3 0.0 copy-start.33
  1.3 0.6 copy-done.33
  2.0 0.6 compare_convert_fusion.live_ref
  2.6 111.4 %edge_step.1 = (f32[1024,256]{1,0:T(8,128)}, f32[1,1024]{1,0:T(1,128)}, s16[1024,256]{1,0:T(8,128)(2,1)S(1)}, f32[2,1024]{1,0:T(2,128)S(1)}) custom-call(f32[1024,256]{1,0:T(8,128)} %dest_ref.1, f32[1,1024]{1,0:T(1,128)} %bitcast.61, f32[1024,256]{1,0:T(8,128)} %source_ref.1, f32[1,1024]{1,0:T(1,128)} %bitcast.62, s32[1,1024]{1,0:T(1,128)} %bitcast.63, ...), custom_call_target="tpu_custom_call" | custom-call | tf_op jit(solution)/shard_map/edge_step/pallas_call | solution.py:411
  114.0 0.0 copy-start.30
  114.0 31.6 %conditional.4 = (f32[2,1024]{1,0:T(2,128)}, f32[1,1024]{1,0:T(1,128)}, f32[1,1024]{1,0:T(1,128)}, f32[1024,1]{0,1:T(1,128)S(1)}, f32[1024]{0:T(1024)S(1)}, /*index=5*/s16[1024,256]{1,0:T(8,128)(2,1)}) conditional(s32[]{:T(128)} %bitcast.39, (f32[2,1024]{1,0:T(2,128)S(1)}, s16[1024,256]{1,0:T(8,128)(2,1)S(1)}) %tuple.145, ...), branch_computations={%region_0.0_spmd, %region_1.0_spmd, %region_2.0_spmd, %region_3.0_... | conditional | bytes 2212024
  114.0 5.5 %collective-permute-start.13 = (s16[1024,256]{1,0:T(8,128)(2,1)S(1)}, s16[1024,256]{1,0:T(8,128)(2,1)}, u32[]{:S(2)}, u32[]{:S(2)}) collective-permute-start(s16[1024,256]{1,0:T(8,128)(2,1)S(1)} %get-tuple-element.93), channel_id=1, source_target_pairs={{0,224},{32,192},{64,160},{96,128},{128,96},{160,64},{192,32},{224... | collective-permute-start | bytes 1572872 | tf_op jit(solution)/shard_map/cond/branch_6_fun/ppermute | solution.py:475
  119.6 1.9 %collective-permute-start.12 = (f32[2,1024]{1,0:T(2,128)S(1)}, f32[2,1024]{1,0:T(2,128)S(1)}, u32[]{:S(2)}, u32[]{:S(2)}) collective-permute-start(f32[2,1024]{1,0:T(2,128)S(1)} %get-tuple-element.92), channel_id=1, source_target_pairs={{0,224},{32,192},{64,160},{96,128},{128,96},{160,64},{192,32},{224... | collective-permute-start | bytes 24584 | tf_op jit(solution)/shard_map/cond/branch_6_fun/ppermute | solution.py:475
  121.5 22.2 %collective-permute-done.12 = f32[2,1024]{1,0:T(2,128)S(1)} collective-permute-done((f32[2,1024]{1,0:T(2,128)S(1)}, f32[2,1024]{1,0:T(2,128)S(1)}, u32[]{:S(2)}, u32[]{:S(2)}) %collective-permute-start.12) | collective-permute-done | bytes 8224 | tf_op jit(solution)/shard_map/cond/branch_6_fun/ppermute | solution.py:475
  143.7 0.0 copy-start.6
  143.7 0.6 fusion.6
  144.3 0.0 copy-done.6
  144.3 0.0 copy-start.21
  144.3 0.6 copy-done.21
  144.9 0.7 copy.55
  145.6 0.0 collective-permute-done.13
  145.6 0.0 copy-start.32
  145.6 0.6 copy-done.32
  146.2 2.2 %convert_multiply_fusion = f32[1024,256]{1,0:T(8,128)} fusion(s16[1024,256]{1,0:T(8,128)(2,1)} %get-tuple-element.135, f32[1024]{0:T(1024)S(1)} %bitcast.58), kind=kLoop, calls=%fused_computation | loop fusion | flops 524288 | bytes 1576960 | tf_op jit(solution)/shard_map/mul | solution.py:480
  148.4 0.0 copy-done.30
  148.4 0.0 copy-start.31
  148.4 1.0 copy.108
  149.4 0.0 copy-done.31
  149.4 0.6 copy.109
  (2 shorter events, 0.0 us)
Async XLA Ops:
  1.3 0.7 copy-start.33
  114.0 34.4 %copy-start.30 = (f32[1024,256]{1,0:T(8,128)S(1)}, f32[1024,256]{1,0:T(8,128)}, u32[]{:S(2)}) copy-start(f32[1024,256]{1,0:T(8,128)} %get-tuple-element.260) | copy-start | bytes 3145732
  114.0 31.6 %collective-permute-start.13 = (s16[1024,256]{1,0:T(8,128)(2,1)S(1)}, s16[1024,256]{1,0:T(8,128)(2,1)}, u32[]{:S(2)}, u32[]{:S(2)}) collective-permute-start(s16[1024,256]{1,0:T(8,128)(2,1)S(1)} %get-tuple-element.93), channel_id=1, source_target_pairs={{0,224},{32,192},{64,160},{96,128},{128,96},{160,64},{192,32},{224... | collective-permute-start | bytes 1572872 | tf_op jit(solution)/shard_map/cond/branch_6_fun/ppermute | solution.py:475
  119.6 24.1 %collective-permute-start.12 = (f32[2,1024]{1,0:T(2,128)S(1)}, f32[2,1024]{1,0:T(2,128)S(1)}, u32[]{:S(2)}, u32[]{:S(2)}) collective-permute-start(f32[2,1024]{1,0:T(2,128)S(1)} %get-tuple-element.92), channel_id=1, source_target_pairs={{0,224},{32,192},{64,160},{96,128},{128,96},{160,64},{192,32},{224... | collective-permute-start | bytes 24584 | tf_op jit(solution)/shard_map/cond/branch_6_fun/ppermute | solution.py:475
  143.7 0.6 copy-start.6
  144.3 0.6 copy-start.21
  145.6 0.6 copy-start.32
  148.4 1.0 copy-start.31
